TPU v7x, 256 devices: a whole 4x4x8 slice. The times are simulated.
256 devices in a mesh: seg: 16 (over z, core), bond: 16 (over x, y).
Axes of the slice: x: 4, y: 4, z: 8, core: 2. Of those that a mesh axis runs over, the one named last changes fastest.
Arguments:
- left_env: bfloat16 [16, 1024, 6, 1024], P('seg', 'bond'), may hold values from -0.1875 to 0.1875
- prev_left: bfloat16 [16, 1024, 1024], P('seg'), may hold values from -0.25 to 1.25
- cur_site: bfloat16 [16, 1024, 4, 1024], P('seg', 'bond'), may hold values from -6 to 6
- prev_site: bfloat16 [16, 1024, 4, 1024], P('seg', None, None, 'bond'), may hold values from -6 to 6
- hamiltonian: bfloat16 [16, 6, 6, 4, 4], P('seg'), may hold values from -1.25 to 1.25
- right_env: bfloat16 [16, 1024, 6, 1024], P('seg', 'bond'), may hold values from -0.078125 to 0.078125
- prev_right: bfloat16 [16, 1024, 1024], P('seg'), may hold values from -0.25 to 1.25
Outputs:
- new_site: bfloat16 [16, 1024, 4, 1024], P('seg', 'bond')
- center: float32 [16, 1024, 1024], P('seg', 'bond')
All inputs are finite; a program needn't handle non-finite values.
Results may differ from a plain program's by a relative error of at most 0.0054.
Values may be sent and summed in bfloat16 or wider, within the bound.
No kernel may reach another device: no remote copies, remote signals or barrier semaphores. Data moves between devices by JAX's collectives and lax.ppermute only.
A program may use at most 128 MiB of HBM per device.

v0:
```python
import math
import jax
import jax.numpy as jnp
from jax import lax
from jax.sharding import PartitionSpec as P

PHYS = 4
MPOB = 6


def shifted(block, axis, distance):
    devices = range(lax.axis_size(axis))
    route = [((i - distance) % len(devices), i) for i in devices]
    return lax.ppermute(block, axis, route)


def shards(left_env, prev_left, cur_site, prev_site, hamiltonian, right_env, prev_right):
    left_now, prev_now = shifted((left_env[0], prev_left[0]), "seg", 1)
    own_rows = left_now.shape[0]
    bond_width = left_now.shape[2]
    coupling = hamiltonian[0].astype(jnp.float32)
    current = lax.all_gather(cur_site[0], "bond", axis=0, tiled=True)
    projected = jnp.dot(
        left_now.reshape(own_rows * MPOB, bond_width),
        current.reshape(bond_width, PHYS * bond_width),
        preferred_element_type=jnp.float32,
    ).reshape(own_rows, MPOB, PHYS, bond_width)
    mixture = jnp.einsum(
        "autc,uvst->asvc", projected, coupling, precision=lax.Precision.HIGHEST
    ).astype(jnp.bfloat16)
    applied = jnp.einsum(
        "asvc,cvy->asy",
        mixture,
        lax.all_gather(right_env[0], "bond", axis=0, tiled=True),
        preferred_element_type=jnp.float32,
    )
    previous = lax.all_gather(prev_site[0], "bond", axis=2, tiled=True)
    own_left = lax.dynamic_slice_in_dim(prev_now, lax.axis_index("bond") * own_rows, own_rows, 0)
    partial_value = jnp.einsum(
        "ab,bsc->asc", own_left, previous, preferred_element_type=jnp.float32
    ).astype(jnp.bfloat16)
    second = jnp.einsum(
        "asc,cy->asy", partial_value, prev_right[0], preferred_element_type=jnp.float32
    )
    target = (2.0 * applied - second).reshape(own_rows * PHYS, bond_width)
    local_correlation = jnp.dot(
        target.T, target, precision=lax.Precision.HIGHEST, preferred_element_type=jnp.float32
    )
    correlation = lax.psum(local_correlation, "bond")
    triangle = jnp.linalg.cholesky(correlation)
    solved = jax.scipy.linalg.solve_triangular(triangle, target.T, lower=True)
    norming = math.sqrt(bond_width * PHYS)
    new_site = (solved.T * norming).astype(jnp.bfloat16).reshape(1, own_rows, PHYS, bond_width)
    offset = lax.axis_index("bond") * own_rows
    center = lax.dynamic_slice_in_dim(triangle.T, offset, own_rows, 0) / norming
    return (new_site, center[None])


def solution(mesh):
    return jax.shard_map(
        shards,
        mesh=mesh,
        in_specs=(
            P("seg", "bond", None, None),
            P("seg", None, None),
            P("seg", "bond", None, None),
            P("seg", None, None, "bond"),
            P("seg", None, None, None, None),
            P("seg", "bond", None, None),
            P("seg", None, None),
        ),
        out_specs=(P("seg", "bond", None, None), P("seg", "bond", None)),
        check_vma=False,
    )
```

profile of v0, /device:TPU:1, one launch (start us, length us, event | category | flops | bytes accessed | tf_op | source)
XLA Modules:
  0.0 756.7 jit_solution(14787921494383537855)
XLA Ops:
  8.0 2.2 copy.56
  11.0 3.0 collective-permute-start
  14.1 75.9 %all-gather.7.cloned.1.call-done = bf16[1,1024,4,1024]{3,2,0,1:T(4,128)(2,1)} async-done(((bf16[1,64,4,1024]{3,2,0,1:T(4,128)(2,1)}), bf16[1,1024,4,1024]{3,2,0,1:T(4,128)(2,1)}) %all-gather.7.cloned.1.call-update) | async-done | bytes 8388624 | tf_op jit(solution)/shard_map/all_gather | solution.py:22
  90.0 13.8 %copy.82 = bf16[1,1024,4,1024]{1,3,2,0:T(8,128)(2,1)} copy(bf16[1,1024,4,1024]{3,2,0,1:T(4,128)(2,1)} %all-gather.7.cloned.1.call-done) | data formatting | bytes 16777216 | tf_op jit(solution)/shard_map/reshape | solution.py:25
  103.9 64.7 %all-gather.11.cloned.1.call-done = bf16[1,1024,4,1024]{1,2,0,3:T(4,128)(2,1)} async-done(((bf16[1,1024,4,64]{1,2,0,3:T(4,128)(2,1)}), bf16[1,1024,4,1024]{1,2,0,3:T(4,128)(2,1)}) %all-gather.11.cloned.1.call-update) | async-done | bytes 8388624 | tf_op jit(solution)/shard_map/all_gather | solution.py:37
  168.6 13.7 %copy.57 = bf16[1,1024,4,1024]{3,1,2,0:T(8,128)(2,1)} copy(bf16[1,1024,4,1024]{1,2,0,3:T(4,128)(2,1)} %all-gather.11.cloned.1.call-done) | data formatting | bytes 16777216 | tf_op jit(solution)/shard_map/all_gather | solution.py:37
  182.3 6.3 fusion.14
  188.6 11.5 %fusion.8 = bf16[64,4,6,1024]{3,2,1,0:T(8,128)(2,1)} fusion(f32[64,6,4,1024,1]{3,0,2,1,4:T(8,128)S(1)} %fusion.14, bf16[1,6,6,4,4]{2,4,3,1,0:T(4,128)(2,1)S(1)} %copy-done.4), kind=kOutput, calls=%fused_computation.11 | convolution fusion | flops 454557696 | bytes 9438336 | tf_op jit(solution)/shard_map/autc,uvst->asvc/dot_general | solution.py:28
  200.2 65.7 %all-gather.9.cloned.1.call-done = bf16[1,1024,6,1024]{3,1,2,0:T(8,128)(2,1)} async-done(((bf16[1,64,6,1024]{3,1,2,0:T(8,128)(2,1)}), bf16[1,1024,6,1024]{3,1,2,0:T(8,128)(2,1)}) %all-gather.9.cloned.1.call-update) | async-done | bytes 12582928 | tf_op jit(solution)/shard_map/all_gather | solution.py:34
  265.9 12.8 %fusion.24 = f32[64,4,1024]{2,0,1:T(8,128)} fusion(bf16[1,1024,6,1024]{3,1,2,0:T(8,128)(2,1)} %all-gather.9.cloned.1.call-done, bf16[64,4,6,1024]{3,2,1,0:T(8,128)(2,1)} %fusion.8), kind=kOutput, calls=%fused_computation.23 | convolution fusion | flops 3221487616 | bytes 16777216 | tf_op jit(solution)/shard_map/asvc,cvy->asy/dot_general | solution.py:31
  278.7 5.8 fusion.29
  284.5 5.1 convolution_bitcast_fusion
  291.1 111.9 %all-reduce.3.cloned.1.call-done = f32[1024,1024]{0,1:T(8,128)} async-done(((f32[1024,1024]{0,1:T(8,128)}), f32[1024,1024]{0,1:T(8,128)}) %all-reduce.3.cloned.1.call-update) | async-done | bytes 4194320 | tf_op jit(solution)/shard_map/psum | solution.py:49
  403.0 5.5 copy.59
  408.5 4.4 fusion.9
  412.9 1.9 copy-done.2
  414.9 11.7 %cholesky.223 = f32[128,128]{1,0:T(8,128)S(1)} custom-call(f32[128,128]{1,0:T(8,128)S(1)} %cholesky.580), custom_call_target="Cholesky" | custom-call | tf_op jit(solution)/shard_map/jit(cholesky)/cholesky | solution.py:50
  426.6 9.8 %custom-call.63 = f32[1,128,128]{1,2,0:T(8,128)S(1)} custom-call(f32[1,128,128]{2,1,0:T(8,128)S(1)} %get-tuple-element.76), custom_call_target="InvertDiagBlocksLowerTriangular" | custom-call | tf_op jit(solution)/shard_map/jit(cholesky)/cholesky | solution.py:50
  440.2 2.5 cholesky.255
  442.7 11.9 %cholesky.244 = f32[128,128]{1,0:T(8,128)S(1)} custom-call(f32[128,128]{1,0:T(8,128)S(1)} %cholesky.584), custom_call_target="Cholesky" | custom-call | tf_op jit(solution)/shard_map/jit(cholesky)/cholesky | solution.py:50
  456.1 9.8 %custom-call.64 = f32[1,128,128]{1,2,0:T(8,128)S(1)} custom-call(f32[1,128,128]{2,1,0:T(8,128)S(1)} %get-tuple-element.73), custom_call_target="InvertDiagBlocksLowerTriangular" | custom-call | tf_op jit(solution)/shard_map/jit(cholesky)/cholesky | solution.py:50
  467.2 2.1 convolution_subtract_fusion.1
  469.3 11.7 %cholesky.468 = f32[128,128]{1,0:T(8,128)S(1)} custom-call(f32[128,128]{1,0:T(8,128)S(1)} %cholesky.589), custom_call_target="Cholesky" | custom-call | tf_op jit(solution)/shard_map/jit(cholesky)/cholesky | solution.py:50
  482.3 9.8 %custom-call.65 = f32[1,128,128]{1,2,0:T(8,128)S(1)} custom-call(f32[1,128,128]{2,1,0:T(8,128)S(1)} %get-tuple-element.70), custom_call_target="InvertDiagBlocksLowerTriangular" | custom-call | tf_op jit(solution)/shard_map/jit(cholesky)/cholesky | solution.py:50
  493.3 2.3 convolution_subtract_fusion.2
  495.6 12.1 %cholesky.487 = f32[128,128]{1,0:T(8,128)S(1)} custom-call(f32[128,128]{1,0:T(8,128)S(1)} %cholesky.594), custom_call_target="Cholesky" | custom-call | tf_op jit(solution)/shard_map/jit(cholesky)/cholesky | solution.py:50
  509.0 9.8 %custom-call.66 = f32[1,128,128]{1,2,0:T(8,128)S(1)} custom-call(f32[1,128,128]{2,1,0:T(8,128)S(1)} %get-tuple-element.67), custom_call_target="InvertDiagBlocksLowerTriangular" | custom-call | tf_op jit(solution)/shard_map/jit(cholesky)/cholesky | solution.py:50
  520.0 2.3 convolution_subtract_fusion.3
  522.3 11.7 %cholesky.506 = f32[128,128]{1,0:T(8,128)S(1)} custom-call(f32[128,128]{1,0:T(8,128)S(1)} %cholesky.599), custom_call_target="Cholesky" | custom-call | tf_op jit(solution)/shard_map/jit(cholesky)/cholesky | solution.py:50
  535.4 10.0 %custom-call.67 = f32[1,128,128]{1,2,0:T(8,128)S(1)} custom-call(f32[1,128,128]{2,1,0:T(8,128)S(1)} %get-tuple-element.64), custom_call_target="InvertDiagBlocksLowerTriangular" | custom-call | tf_op jit(solution)/shard_map/jit(cholesky)/cholesky | solution.py:50
  546.4 2.3 convolution_subtract_fusion.4
  548.7 11.7 %cholesky.526 = f32[128,128]{1,0:T(8,128)S(1)} custom-call(f32[128,128]{1,0:T(8,128)S(1)} %cholesky.604), custom_call_target="Cholesky" | custom-call | tf_op jit(solution)/shard_map/jit(cholesky)/cholesky | solution.py:50
  561.7 9.8 %custom-call.68 = f32[1,128,128]{1,2,0:T(8,128)S(1)} custom-call(f32[1,128,128]{2,1,0:T(8,128)S(1)} %get-tuple-element.61), custom_call_target="InvertDiagBlocksLowerTriangular" | custom-call | tf_op jit(solution)/shard_map/jit(cholesky)/cholesky | solution.py:50
  572.4 2.0 convolution_subtract_fusion.11
  574.5 11.9 %cholesky.546 = f32[128,128]{1,0:T(8,128)S(1)} custom-call(f32[128,128]{1,0:T(8,128)S(1)} %cholesky.609), custom_call_target="Cholesky" | custom-call | tf_op jit(solution)/shard_map/jit(cholesky)/cholesky | solution.py:50
  587.6 9.8 %custom-call.69 = f32[1,128,128]{1,2,0:T(8,128)S(1)} custom-call(f32[1,128,128]{2,1,0:T(8,128)S(1)} %get-tuple-element.58), custom_call_target="InvertDiagBlocksLowerTriangular" | custom-call | tf_op jit(solution)/shard_map/jit(cholesky)/cholesky | solution.py:50
  600.1 11.7 %cholesky.564 = f32[128,128]{1,0:T(8,128)S(1)} custom-call(f32[128,128]{1,0:T(8,128)S(1)} %convolution_subtract_fusion.13), custom_call_target="Cholesky" | custom-call | tf_op jit(solution)/shard_map/jit(cholesky)/cholesky | solution.py:50
  618.8 6.6 fusion.10
  625.3 27.4 %while.1 = (s32[]{:T(128)}, f32[1024,1024]{1,0:T(8,128)}, s32[8,2]{0,1:T(2,128)S(1)}, f32[8,128,128]{2,1,0:T(8,128)}, s32[]{:T(128)}) while((s32[]{:T(128)}, f32[1024,1024]{1,0:T(8,128)}, s32[8,2]{0,1:T(2,128)S(1)}, f32[8,128,128]{2,1,0:T(8,128)}, s32[]{:T(128)}) %tuple.65), condition=%wide.while_cond, body=%wide.while_body.sunk | while | flops 2 | bytes 132705 | solution.py:51
  625.9 2.8 bitcast_dynamic-update-slice_fusion.2
  629.4 2.8 bitcast_dynamic-update-slice_fusion.2
  632.8 2.8 bitcast_dynamic-update-slice_fusion.2
  636.2 2.8 bitcast_dynamic-update-slice_fusion.2
  639.6 2.8 bitcast_dynamic-update-slice_fusion.2
  643.1 2.8 bitcast_dynamic-update-slice_fusion.2
  646.5 2.8 bitcast_dynamic-update-slice_fusion.2
  649.9 2.8 bitcast_dynamic-update-slice_fusion.2
  652.7 79.6 %custom-call.70 = f32[8,128,128]{1,2,0:T(8,128)S(1)} custom-call(f32[8,128,128]{2,1,0:T(8,128)} %get-tuple-element.9), custom_call_target="InvertDiagBlocksLowerTriangular" | custom-call | tf_op jit(solution)/shard_map/jit(_solve_triangular)/triangular_solve | solution.py:51
  (95 shorter events, 47.1 us)
Async XLA Ops:
  7.2 271.5 %copy-start = (bf16[1,1024,1024]{2,1,0:T(8,128)(2,1)S(1)}, bf16[1,1024,1024]{2,1,0:T(8,128)(2,1)}, u32[]{:S(2)}) copy-start(bf16[1,1024,1024]{2,1,0:T(8,128)(2,1)} %param.13) | copy-start | bytes 6291460
  7.2 82.9 %all-gather.7.cloned.1.call-start = ((), (), s32[]{:S(2)}) async-start(), calls=%async_computation.1 | async-start | bytes 8912896 | tf_op jit(solution)/shard_map/all_gather | solution.py:22
  7.9 160.7 %all-gather.11.cloned.1.call-start = ((), (), s32[]{:S(2)}) async-start(), calls=%async_computation.3 | async-start | bytes 8912896 | tf_op jit(solution)/shard_map/all_gather | solution.py:37
  10.2 255.6 %all-gather.9.cloned.1.call-start = ((), (), s32[]{:S(2)}) async-start(), calls=%async_computation.2 | async-start | bytes 13369344 | tf_op jit(solution)/shard_map/all_gather | solution.py:34
  11.0 392.0 %all-reduce.3.cloned.1.call-start = ((), (), s32[]{:S(2)}) async-start(), calls=%async_computation | async-start | bytes 8388608 | tf_op jit(solution)/shard_map/psum | solution.py:49
  11.0 171.3 %collective-permute-start = (bf16[64,6,1024]{2,0,1:T(8,128)(2,1)}, bf16[64,6,1024]{2,0,1:T(8,128)(2,1)S(1)}, u32[]{:S(2)}, u32[]{:S(2)}) collective-permute-start(bf16[64,6,1024]{2,0,1:T(8,128)(2,1)} %bitcast.185), channel_id=1, source_target_pairs={{240,0},{0,16},{16,32},{32,48},{48,64},{64,80},{80,96},{96,112},{1... | collective-permute-start | bytes 2359304 | tf_op jit(solution)/shard_map/ppermute | solution.py:14
  14.1 264.6 %collective-permute-start.1 = (bf16[1024,1024]{1,0:T(8,128)(2,1)}, bf16[1024,1024]{1,0:T(8,128)(2,1)}, u32[]{:S(2)}, u32[]{:S(2)}) collective-permute-start(bf16[1024,1024]{1,0:T(8,128)(2,1)} %bitcast.184), channel_id=1, source_target_pairs={{240,0},{0,16},{16,32},{32,48},{48,64},{64,80},{80,96},{96,112},{1... | collective-permute-start | bytes 6291464 | tf_op jit(solution)/shard_map/ppermute | solution.py:14
  182.3 6.3 copy-start.4
  412.9 1.9 copy-start.2
  732.3 8.1 %copy-start.3 = (f32[8,128,128]{1,2,0:T(8,128)}, f32[8,128,128]{1,2,0:T(8,128)S(1)}, u32[]{:S(2)}) copy-start(f32[8,128,128]{1,2,0:T(8,128)S(1)} %custom-call.70) | copy-start | bytes 1572868
  740.8 9.1 %copy-start.1 = (bf16[1,1024,1024]{2,1,0:T(8,128)(2,1)S(1)}, bf16[1,1024,1024]{2,1,0:T(8,128)(2,1)}, u32[]{:S(2)}) copy-start(bf16[1,1024,1024]{2,1,0:T(8,128)(2,1)} %param.13) | copy-start | bytes 6291460
Sparse Core Ops, SparseCore 0:
  10.4 79.5 all-gather.6
  93.0 75.4 all-gather.10
  171.1 94.7 all-gather.8
  289.8 113.1 all-reduce.2
where the time goes:
time: 764 us; the launch traced here: 757 us
  waiting for transfers between devices  320 us (42%)
  other arithmetic  264 us (35%)
  matrix products  78.2 us (10%)
  local copies, waits for them, and re-layouts  71.6 us (9%)
  between operations  19.4 us (3%)
    another operation x30, other arithmetic, shards(): triangle = jnp.linalg.cholesky(correlation)  172 us
    psum x1, waiting for transfers between devices, shards(): correlation = lax.psum(local_correlation, 'bond')  112 us
    another operation x3, other arithmetic, shards(): solved = jax.scipy.linalg.solve_triangular(triangle, target.T, lower=True)  86.2 us
    all_gather x1, waiting for transfers between devices, shards(): current = lax.all_gather(cur_site[0], 'bond', axis=0, tiled=True)  75.9 us
    all_gather x1, waiting for transfers between devices, shards(): lax.all_gather(right_env[0], 'bond', axis=0, tiled=True)  65.7 us
    all_gather x1, waiting for transfers between devices, shards(): previous = lax.all_gather(prev_site[0], 'bond', axis=2, tiled=True)  64.7 us
    another operation x24, local copies, waits for them, and re-layouts  27.4 us
    another operation x14, matrix products, shards(): triangle = jnp.linalg.cholesky(correlation)  22.7 us
  transfers between devices with their start and end apart: 6, of which 4 were waited for; matrix products, arithmetic and copies ran while one was open for 8% of the time, Pallas kernels for 0%

commit v1 on v0

--- a/solution.py
+++ b/solution.py
@@ -46,7 +46,7 @@
     local_correlation = jnp.dot(
         target.T, target, precision=lax.Precision.HIGHEST, preferred_element_type=jnp.float32
     )
-    correlation = lax.psum(local_correlation, "bond")
+    correlation = jnp.sum(lax.all_gather(local_correlation, "bond"), axis=0)
     triangle = jnp.linalg.cholesky(correlation)
     solved = jax.scipy.linalg.solve_triangular(triangle, target.T, lower=True)
     norming = math.sqrt(bond_width * PHYS)

time: 764 us -> 1050 us (1.37)
  waiting for transfers between devices: 320 us -> 580 us
  other arithmetic: 264 us -> 287 us
    all_gather x0 -> x1, waiting for transfers between devices: none -> 372 us  [shards(): correlation = jnp.sum(lax.all_gather(local_correlation, 'bond'), axis=0)]
    psum x1 -> x0, waiting for transfers between devices: 112 us -> none  [shards(): correlation = lax.psum(local_correlation, 'bond')]
    reduce_sum x0 -> x1, other arithmetic: none -> 22.9 us  [shards(): correlation = jnp.sum(lax.all_gather(local_correlation, 'bond'), axis=0)]
  transfers between devices with their start and end apart: 6 -> 6, of which waited for: 4 -> 4; matrix products, arithmetic and copies ran while one was open for 8% -> 6% of each run, Pallas kernels for 0% -> 0%
where the time goes in v1:
time: 1050 us; the launch traced here: 1040 us
  waiting for transfers between devices  580 us (55%)
  other arithmetic  287 us (27%)
  matrix products  78.2 us (7%)
  local copies, waits for them, and re-layouts  71.6 us (7%)
  between operations  19.4 us (2%)
    all_gather x1, waiting for transfers between devices, shards(): correlation = jnp.sum(lax.all_gather(local_correlation, 'bond'), axis=0)  372 us
    another operation x30, other arithmetic, shards(): triangle = jnp.linalg.cholesky(correlation)  172 us
    another operation x3, other arithmetic, shards(): solved = jax.scipy.linalg.solve_triangular(triangle, target.T, lower=True)  86.2 us
    all_gather x1, waiting for transfers between devices, shards(): current = lax.all_gather(cur_site[0], 'bond', axis=0, tiled=True)  75.9 us
    all_gather x1, waiting for transfers between devices, shards(): lax.all_gather(right_env[0], 'bond', axis=0, tiled=True)  65.7 us
    all_gather x1, waiting for transfers between devices, shards(): previous = lax.all_gather(prev_site[0], 'bond', axis=2, tiled=True)  64.7 us
    another operation x24, local copies, waits for them, and re-layouts  27.3 us
    reduce_sum x1, other arithmetic, shards(): correlation = jnp.sum(lax.all_gather(local_correlation, 'bond'), axis=0)  22.9 us
  transfers between devices with their start and end apart: 6, of which 4 were waited for; matrix products, arithmetic and copies ran while one was open for 6% of the time, Pallas kernels for 0%

profile of v1, /device:TPU:1, one launch (start us, length us, event | category | flops | bytes accessed | tf_op | source)
XLA Modules:
  0.0 1039.7 jit_solution(12966754765764836906)
XLA Ops:
  8.0 2.2 copy.53
  11.0 3.0 collective-permute-start
  14.1 75.9 %all-gather.9.cloned.1.call-done = bf16[1,1024,4,1024]{3,2,0,1:T(4,128)(2,1)} async-done(((bf16[1,64,4,1024]{3,2,0,1:T(4,128)(2,1)}), bf16[1,1024,4,1024]{3,2,0,1:T(4,128)(2,1)}) %all-gather.9.cloned.1.call-update) | async-done | bytes 8388624 | tf_op jit(solution)/shard_map/all_gather | solution.py:22
  90.0 13.8 %copy.77 = bf16[1,1024,4,1024]{1,3,2,0:T(8,128)(2,1)} copy(bf16[1,1024,4,1024]{3,2,0,1:T(4,128)(2,1)} %all-gather.9.cloned.1.call-done) | data formatting | bytes 16777216 | tf_op jit(solution)/shard_map/reshape | solution.py:25
  103.9 64.7 %all-gather.13.cloned.1.call-done = bf16[1,1024,4,1024]{1,2,0,3:T(4,128)(2,1)} async-done(((bf16[1,1024,4,64]{1,2,0,3:T(4,128)(2,1)}), bf16[1,1024,4,1024]{1,2,0,3:T(4,128)(2,1)}) %all-gather.13.cloned.1.call-update) | async-done | bytes 8388624 | tf_op jit(solution)/shard_map/all_gather | solution.py:37
  168.6 13.7 %copy.54 = bf16[1,1024,4,1024]{3,1,2,0:T(8,128)(2,1)} copy(bf16[1,1024,4,1024]{1,2,0,3:T(4,128)(2,1)} %all-gather.13.cloned.1.call-done) | data formatting | bytes 16777216 | tf_op jit(solution)/shard_map/all_gather | solution.py:37
  182.3 6.3 fusion.14
  188.6 11.5 %fusion.8 = bf16[64,4,6,1024]{3,2,1,0:T(8,128)(2,1)} fusion(f32[64,6,4,1024,1]{3,0,2,1,4:T(8,128)S(1)} %fusion.14, bf16[1,6,6,4,4]{2,4,3,1,0:T(4,128)(2,1)S(1)} %copy-done.4), kind=kOutput, calls=%fused_computation.11 | convolution fusion | flops 454557696 | bytes 9438336 | tf_op jit(solution)/shard_map/autc,uvst->asvc/dot_general | solution.py:28
  200.2 65.7 %all-gather.11.cloned.1.call-done = bf16[1,1024,6,1024]{3,1,2,0:T(8,128)(2,1)} async-done(((bf16[1,64,6,1024]{3,1,2,0:T(8,128)(2,1)}), bf16[1,1024,6,1024]{3,1,2,0:T(8,128)(2,1)}) %all-gather.11.cloned.1.call-update) | async-done | bytes 12582928 | tf_op jit(solution)/shard_map/all_gather | solution.py:34
  265.9 12.8 %fusion.24 = f32[64,4,1024]{2,0,1:T(8,128)} fusion(bf16[1,1024,6,1024]{3,1,2,0:T(8,128)(2,1)} %all-gather.11.cloned.1.call-done, bf16[64,4,6,1024]{3,2,1,0:T(8,128)(2,1)} %fusion.8), kind=kOutput, calls=%fused_computation.23 | convolution fusion | flops 3221487616 | bytes 16777216 | tf_op jit(solution)/shard_map/asvc,cvy->asy/dot_general | solution.py:31
  278.7 5.8 fusion.29
  284.5 5.1 convolution_bitcast_fusion
  291.0 372.1 %all-gather.15.cloned.1.call-done = f32[16384,1024]{1,0:T(8,128)} async-done(((f32[1024,1024]{1,0:T(8,128)}), f32[16384,1024]{1,0:T(8,128)}) %all-gather.15.cloned.1.call-update) | async-done | bytes 67108880 | tf_op jit(solution)/shard_map/all_gather | solution.py:49
  663.1 22.9 %reduce_sum.9 = f32[1024,1024]{1,0:T(8,128)} reduce(f32[16,1024,1024]{2,1,0:T(8,128)} %bitcast.24, f32[]{:T(128)} %constant.282.clone.1), dimensions={0}, to_apply=%region_0.0 | reduce | flops 15728640 | bytes 71303168 | tf_op jit(solution)/shard_map/reduce_sum | solution.py:49
  686.1 5.5 copy.55
  691.6 4.4 fusion.9
  698.0 11.7 %cholesky.223 = f32[128,128]{1,0:T(8,128)S(1)} custom-call(f32[128,128]{1,0:T(8,128)S(1)} %cholesky.580), custom_call_target="Cholesky" | custom-call | tf_op jit(solution)/shard_map/jit(cholesky)/cholesky | solution.py:50
  709.7 2.5 cholesky.255
  712.2 9.8 custom-call.63
  725.8 11.9 %cholesky.244 = f32[128,128]{1,0:T(8,128)S(1)} custom-call(f32[128,128]{1,0:T(8,128)S(1)} %cholesky.584), custom_call_target="Cholesky" | custom-call | tf_op jit(solution)/shard_map/jit(cholesky)/cholesky | solution.py:50
  739.2 9.8 custom-call.64
  750.3 2.1 convolution_subtract_fusion.1
  752.4 11.7 %cholesky.468 = f32[128,128]{1,0:T(8,128)S(1)} custom-call(f32[128,128]{1,0:T(8,128)S(1)} %cholesky.589), custom_call_target="Cholesky" | custom-call | tf_op jit(solution)/shard_map/jit(cholesky)/cholesky | solution.py:50
  765.4 9.8 custom-call.65
  776.4 2.3 convolution_subtract_fusion.2
  778.7 12.1 %cholesky.487 = f32[128,128]{1,0:T(8,128)S(1)} custom-call(f32[128,128]{1,0:T(8,128)S(1)} %cholesky.594), custom_call_target="Cholesky" | custom-call | tf_op jit(solution)/shard_map/jit(cholesky)/cholesky | solution.py:50
  792.1 9.8 custom-call.66
  803.0 2.3 convolution_subtract_fusion.3
  805.4 11.7 %cholesky.506 = f32[128,128]{1,0:T(8,128)S(1)} custom-call(f32[128,128]{1,0:T(8,128)S(1)} %cholesky.599), custom_call_target="Cholesky" | custom-call | tf_op jit(solution)/shard_map/jit(cholesky)/cholesky | solution.py:50
  818.5 10.0 custom-call.67
  829.5 2.3 convolution_subtract_fusion.4
  831.8 11.7 %cholesky.526 = f32[128,128]{1,0:T(8,128)S(1)} custom-call(f32[128,128]{1,0:T(8,128)S(1)} %cholesky.604), custom_call_target="Cholesky" | custom-call | tf_op jit(solution)/shard_map/jit(cholesky)/cholesky | solution.py:50
  844.8 9.8 custom-call.68
  855.5 2.0 convolution_subtract_fusion.11
  857.6 11.9 %cholesky.546 = f32[128,128]{1,0:T(8,128)S(1)} custom-call(f32[128,128]{1,0:T(8,128)S(1)} %cholesky.609), custom_call_target="Cholesky" | custom-call | tf_op jit(solution)/shard_map/jit(cholesky)/cholesky | solution.py:50
  870.7 9.8 custom-call.69
  883.2 11.7 %cholesky.564 = f32[128,128]{1,0:T(8,128)S(1)} custom-call(f32[128,128]{1,0:T(8,128)S(1)} %convolution_subtract_fusion.13), custom_call_target="Cholesky" | custom-call | tf_op jit(solution)/shard_map/jit(cholesky)/cholesky | solution.py:50
  901.8 6.6 fusion.10
  908.4 27.4 %while.1 = (s32[]{:T(128)}, f32[1024,1024]{1,0:T(8,128)}, s32[8,2]{0,1:T(2,128)S(1)}, f32[8,128,128]{2,1,0:T(8,128)}, s32[]{:T(128)}) while((s32[]{:T(128)}, f32[1024,1024]{1,0:T(8,128)}, s32[8,2]{0,1:T(2,128)S(1)}, f32[8,128,128]{2,1,0:T(8,128)}, s32[]{:T(128)}) %tuple.65), condition=%wide.while_cond, body=%wide.while_body.sunk | while | flops 2 | bytes 132705 | solution.py:51
  909.0 2.8 bitcast_dynamic-update-slice_fusion.2
  912.5 2.8 bitcast_dynamic-update-slice_fusion.2
  915.9 2.8 bitcast_dynamic-update-slice_fusion.2
  919.3 2.8 bitcast_dynamic-update-slice_fusion.2
  922.7 2.8 bitcast_dynamic-update-slice_fusion.2
  926.2 2.8 bitcast_dynamic-update-slice_fusion.2
  929.6 2.8 bitcast_dynamic-update-slice_fusion.2
  933.0 2.8 bitcast_dynamic-update-slice_fusion.2
  935.8 79.6 %custom-call.70 = f32[8,128,128]{1,2,0:T(8,128)S(1)} custom-call(f32[8,128,128]{2,1,0:T(8,128)} %get-tuple-element.9), custom_call_target="InvertDiagBlocksLowerTriangular" | custom-call | tf_op jit(solution)/shard_map/jit(_solve_triangular)/triangular_solve | solution.py:51
  (96 shorter events, 49.0 us)
Async XLA Ops:
  7.2 271.5 %copy-start = (bf16[1,1024,1024]{2,1,0:T(8,128)(2,1)S(1)}, bf16[1,1024,1024]{2,1,0:T(8,128)(2,1)}, u32[]{:S(2)}) copy-start(bf16[1,1024,1024]{2,1,0:T(8,128)(2,1)} %param.13) | copy-start | bytes 6291460
  7.2 82.9 %all-gather.9.cloned.1.call-start = ((), (), s32[]{:S(2)}) async-start(), calls=%async_computation | async-start | bytes 8912896 | tf_op jit(solution)/shard_map/all_gather | solution.py:22
  7.9 160.7 %all-gather.13.cloned.1.call-start = ((), (), s32[]{:S(2)}) async-start(), calls=%async_computation.2 | async-start | bytes 8912896 | tf_op jit(solution)/shard_map/all_gather | solution.py:37
  10.2 255.6 %all-gather.11.cloned.1.call-start = ((), (), s32[]{:S(2)}) async-start(), calls=%async_computation.1 | async-start | bytes 13369344 | tf_op jit(solution)/shard_map/all_gather | solution.py:34
  11.0 652.2 %all-gather.15.cloned.1.call-start = ((), (), s32[]{:S(2)}) async-start(), calls=%async_computation.3 | async-start | bytes 71303168 | tf_op jit(solution)/shard_map/all_gather | solution.py:49
  11.0 171.3 %collective-permute-start = (bf16[64,6,1024]{2,0,1:T(8,128)(2,1)}, bf16[64,6,1024]{2,0,1:T(8,128)(2,1)S(1)}, u32[]{:S(2)}, u32[]{:S(2)}) collective-permute-start(bf16[64,6,1024]{2,0,1:T(8,128)(2,1)} %bitcast.186), channel_id=1, source_target_pairs={{240,0},{0,16},{16,32},{32,48},{48,64},{64,80},{80,96},{96,112},{1... | collective-permute-start | bytes 2359304 | tf_op jit(solution)/shard_map/ppermute | solution.py:14
  14.1 264.6 %collective-permute-start.1 = (bf16[1024,1024]{1,0:T(8,128)(2,1)}, bf16[1024,1024]{1,0:T(8,128)(2,1)}, u32[]{:S(2)}, u32[]{:S(2)}) collective-permute-start(bf16[1024,1024]{1,0:T(8,128)(2,1)} %bitcast.185), channel_id=1, source_target_pairs={{240,0},{0,16},{16,32},{32,48},{48,64},{64,80},{80,96},{96,112},{1... | collective-permute-start | bytes 6291464 | tf_op jit(solution)/shard_map/ppermute | solution.py:14
  182.3 6.3 copy-start.4
  696.0 1.9 copy-start.2
  1015.4 8.1 copy-start.3
  1023.9 9.1 copy-start.1
Sparse Core Ops, SparseCore 0:
  10.4 79.5 all-gather.8
  93.0 75.4 all-gather.12
  171.1 94.7 all-gather.10
  289.7 373.3 all-gather.14
